TPU v7x, 256 devices: a whole 4x4x8 slice. The times are simulated.
256 devices in a mesh: layer: 16 (over z, core), vocab: 16 (over x, y).
Axes of the slice: x: 4, y: 4, z: 8, core: 2. Of those that a mesh axis runs over, the one named last changes fastest.
Arguments:
- hidden: bfloat16 [16, 32, 2880], P('layer'), may hold values from -6 to 6
- translator: bfloat16 [16, 2880, 2880], P('layer', None, 'vocab'), may hold values from -0.109375 to 0.109375
- bias: float32 [16, 2880], P('layer', 'vocab'), may hold values from -3 to 3
- gain: float32 [2880], P('vocab'), may hold values from 0.1 to 1.9
- unembed: bfloat16 [2880, 200704], P(None, ('layer', 'vocab')), may hold values from -0.3125 to 0.3125
- final_logits: bfloat16 [32, 200704], P(None, ('layer', 'vocab')), may hold values from -230 to 230
Outputs:
- grad_translator: float32 [16, 2880, 2880], P('layer', None, 'vocab')
- grad_bias: float32 [16, 2880], P('layer', 'vocab')
All inputs are finite; a program needn't handle non-finite values.
Results may differ from a plain program's by a relative error of at most 0.025.
Values may be sent and summed in bfloat16 or wider, within the bound.
A program may use at most 64 MiB of HBM per device.

v0:
```python
import jax
import jax.numpy as jnp
from jax import lax
from jax.sharding import PartitionSpec as P

eps = 1e-05


def from_behind(value, axis, steps):
    count = lax.axis_size(axis)
    first, last = (max(0, -steps), min(count, count - steps))
    return lax.ppermute(value, axis, [(source, source + steps) for source in range(first, last)])


def stats_narrow(final_f32, logits):
    local_top = jnp.max(final_f32, axis=1)
    lens_total = jnp.sum(jnp.exp(logits), axis=1)
    row_top = lax.pmax(local_top, "vocab")
    final_total, lens_sum = lax.psum(
        (jnp.sum(jnp.exp(final_f32 - row_top[:, None]), axis=1), lens_total), "vocab"
    )
    return (row_top + jnp.log(final_total), jnp.log(lens_sum))


def on_device(hidden, translator, bias, gain, unembed, final_logits):
    n_vocab = lax.axis_size("vocab")
    n_layer = lax.axis_size("layer")
    states = hidden[0]
    row_count = states.shape[0]
    model_width = states.shape[1]
    col_count = translator.shape[2]
    col_start = lax.axis_index("vocab") * col_count
    own_states = lax.dynamic_slice_in_dim(states, col_start, col_count, 1).astype(jnp.float32)
    lens_out = (
        own_states
        + jnp.dot(states, translator[0], preferred_element_type=jnp.float32)
        + bias[0][None, :]
    )
    squares = lax.psum(jnp.sum(lens_out * lens_out, axis=1), "vocab")
    inv_rms = lax.rsqrt(squares / model_width + eps)
    normed = (lens_out * inv_rms[:, None] * gain[None, :]).astype(jnp.bfloat16)
    gathered = lax.all_gather(normed[None], ("layer", "vocab"), axis=0, tiled=True)
    gathered = gathered.reshape(n_layer, n_vocab, row_count, col_count)
    unembed_blocks = unembed.reshape(n_vocab, col_count, unembed.shape[1])
    logits = jnp.einsum(
        "lvrd,vdc->lrc", gathered, unembed_blocks, preferred_element_type=jnp.float32
    )
    own_logits = lax.all_to_all(logits, "layer", split_axis=0, concat_axis=2, tiled=True)[0]
    final_f32 = lax.all_gather(final_logits, "layer", axis=1, tiled=True).astype(jnp.float32)
    final_lse, lens_lse = stats_narrow(final_f32, own_logits)
    after_logits, after_lse = from_behind((own_logits, lens_lse), "layer", -1)
    lens_prob = jnp.exp(own_logits - lens_lse[:, None])
    next_prob = jnp.exp(after_logits - after_lse[:, None])
    final_prob = jnp.exp(final_f32 - final_lse[:, None])
    weight = (lax.axis_index("layer") < n_layer - 1).astype(jnp.float32)
    grad_bf = (lens_prob - final_prob + weight * (lens_prob - next_prob)).astype(jnp.bfloat16)
    grad_tiles = lax.all_to_all(grad_bf[None], "layer", split_axis=2, concat_axis=0, tiled=True)
    partial_value = jnp.einsum(
        "lrc,vdc->lvrd", grad_tiles, unembed_blocks, preferred_element_type=jnp.float32
    )
    by_layer = lax.psum_scatter(
        partial_value.astype(jnp.bfloat16), "layer", scatter_dimension=0, tiled=True
    )
    grad_normed = lax.psum_scatter(by_layer, "vocab", scatter_dimension=1, tiled=True).astype(
        jnp.float32
    )[0, 0]
    proj = lax.psum(jnp.sum(gain[None, :] * grad_normed * lens_out, axis=1), "vocab")
    cubed = inv_rms * inv_rms * inv_rms
    grad_out = (
        inv_rms[:, None] * gain[None, :] * grad_normed
        - lens_out * (cubed * proj / model_width)[:, None]
    )
    grad_translator = jnp.einsum(
        "rd,rc->dc", states, grad_out.astype(jnp.bfloat16), preferred_element_type=jnp.float32
    )
    grad_bias = jnp.sum(grad_out, axis=0)
    return (grad_translator[None], grad_bias[None])


def solution(mesh):
    placed = (
        P("layer", None, None),
        P("layer", None, "vocab"),
        P("layer", "vocab"),
        P("vocab"),
        P(None, ("layer", "vocab")),
        P(None, ("layer", "vocab")),
    )
    return jax.shard_map(
        on_device,
        mesh=mesh,
        in_specs=placed,
        out_specs=(P("layer", None, "vocab"), P("layer", "vocab")),
        check_vma=False,
    )
```

profile of v0, /device:TPU:2, one launch (start us, length us, event | category | flops | bytes accessed | tf_op | source)
XLA Modules:
  0.0 680.5 jit_solution(2444177175690705709)
XLA Ops:
  7.2 0.0 copy-start
  7.2 0.0 all-gather.4.cloned.1.call-start
  7.2 1.2 copy-done
  8.4 1.5 multiply_reduce_fusion
  9.9 34.6 %psum.28 = f32[32]{0:T(128)S(1)} all-reduce(f32[32]{0:T(128)S(1)} %get-tuple-element.10), channel_id=1, replica_groups=mesh['layer'=16,'vocab'=16] {'vocab'}, use_global_device_ids=true, to_apply=%region_1.0 | all-reduce | flops 32 | bytes 256 | tf_op jit(solution)/shard_map/psum | solution.py:39
  44.5 1.4 multiply_convert_fusion
  45.9 0.0 all-gather.4.cloned.1.call-update
  45.9 0.0 reduce-scatter.6.cloned.1.call-start
  45.9 7.4 %copy.16 = bf16[2880,784]{1,0:T(8,128)(2,1)} copy(bf16[2880,784]{0,1:T(8,128)(2,1)} %param.10) | data formatting | bytes 9031680 | tf_op args[4]
  53.4 7.4 %reshape.30 = bf16[16,180,784,1]{2,1,0,3:T(8,128)(2,1)} reshape(bf16[2880,784]{1,0:T(8,128)(2,1)} %copy.16) | data formatting | bytes 9031680 | tf_op jit(solution)/shard_map/reshape | solution.py:44
  60.7 104.4 %all-gather.4.cloned.1.call-done = bf16[8192,180]{1,0:T(8,128)(2,1)} async-done(((bf16[32,180]{1,0:T(8,128)(2,1)}), bf16[8192,180]{1,0:T(8,128)(2,1)}) %all-gather.4.cloned.1.call-update) | async-done | bytes 2949136 | tf_op jit(solution)/shard_map/all_gather | solution.py:42
  165.1 6.9 %convolution_bitcast_fusion.1 = f32[16,32,784]{2,1,0:T(8,128)S(1)} fusion(bf16[16,16,32,180]{3,2,1,0:T(8,128)(2,1)} %bitcast.81, bf16[16,180,784,1]{2,1,0,3:T(8,128)(2,1)} %reshape.30), kind=kOutput, calls=%fused_computation.7 | convolution fusion | flops 2312110080 | bytes 9070592 | tf_op jit(solution)/shard_map/lvrd,vdc->lrc/dot_general | solution.py:45
  172.0 49.0 %all_to_all.33 = f32[16,32,784]{2,1,0:T(8,128)S(1)} all-to-all(f32[16,32,784]{2,1,0:T(8,128)S(1)} %convolution_bitcast_fusion.1), channel_id=1, replica_groups=mesh['layer'=16,'vocab'=16] {'layer'}, dimensions={0} | all-to-all | bytes 3211264 | tf_op jit(solution)/shard_map/all_to_all | solution.py:48
  221.1 2.3 copy.17
  223.4 3.2 squeeze.17
  226.5 1.3 collective-permute-start
  227.8 0.0 copy-done.3
  227.8 36.1 %all-gather.1 = bf16[16,784,32]{1,2,0:T(8,128)(2,1)} all-gather(bf16[1,784,32]{1,2,0:T(8,128)(2,1)S(1)} %bitcast.78), channel_id=1, replica_groups=mesh['layer'=16,'vocab'=16] {'layer'}, dimensions={0}, use_global_device_ids=true | all-gather | bytes 852992 | tf_op jit(solution)/shard_map/all_gather | solution.py:49
  263.9 1.4 reduce_max.14
  265.3 33.3 %pmax.7 = f32[32]{0:T(128)S(1)} all-reduce(bf16[32]{0:T(256)(128)(2,1)S(1)} %reduce_max.14), channel_id=1, replica_groups=mesh['layer'=16,'vocab'=16] {'vocab'}, use_global_device_ids=true, to_apply=%region_5.0 | all-reduce | flops 32 | bytes 192 | tf_op jit(solution)/shard_map/pmax | solution.py:18
  298.7 2.7 copy.18
  301.4 3.2 reshape.29
  304.5 1.8 exponential_reduce_fusion.1
  306.3 0.4 exponential_reduce_fusion
  306.7 35.0 %all-reduce.1 = (f32[32]{0:T(128)S(1)}, f32[32]{0:T(128)S(1)}) all-reduce(f32[32]{0:T(128)S(1)} %exponential_reduce_fusion, f32[32]{0:T(128)S(1)} %exponential_reduce_fusion.1), channel_id=1, replica_groups=mesh['layer'=16,'vocab'=16] {'vocab'}, use_global_device_ids=true, to_apply=%region_3.0 | all-reduce | flops 64 | bytes 512 | tf_op jit(solution)/shard_map/psum | solution.py:19
  341.7 1.5 collective-permute-start.1
  343.2 1.5 collective-permute-done.1
  344.7 0.0 collective-permute-done
  344.7 3.2 fusion.6
  347.9 9.9 %copy.19 = bf16[1,32,12544]{1,0,2:T(2,128)(2,1)} copy(bf16[1,32,12544]{2,1,0:T(8,128)(2,1)S(1)} %fusion.6) | data formatting | bytes 1605632 | tf_op jit(solution)/shard_map/broadcast_in_dim | solution.py:57
  357.8 0.5 broadcast.23
  358.3 70.2 %reduce.5 = bf16[12544,32]{1,0:T(8,128)(2,1)} reduce(bf16[12544,1,32]{2,1,0:T(2,128)(2,1)} %bitcast.75, bf16[]{:T(256)} %broadcast.23), dimensions={1}, to_apply=%bitcast.66.reduce_sub_computation | reduce | bytes 1605634
  428.5 4.9 reshape.37
  433.3 29.2 %all_to_all.34 = bf16[16,2,12544]{2,1,0:T(2,128)(2,1)S(1)} all-to-all(bf16[16,2,12544]{2,1,0:T(2,128)(2,1)S(1)} %reshape.37), channel_id=1, replica_groups=mesh['layer'=16,'vocab'=16] {'layer'}, dimensions={0} | all-to-all | bytes 1605632 | tf_op jit(solution)/shard_map/all_to_all | solution.py:57
  462.5 8.4 %reshape.38 = bf16[12544,1,32]{2,1,0:T(2,128)(2,1)} reshape(bf16[16,2,12544]{2,1,0:T(2,128)(2,1)S(1)} %all_to_all.34) | data formatting | bytes 1605632
  470.9 11.6 %copy.20 = bf16[1,32,12544]{2,1,0:T(8,128)(2,1)S(1)} copy(bf16[1,32,12544]{1,0,2:T(2,128)(2,1)} %bitcast.76) | data formatting | bytes 1605632 | tf_op jit(solution)/shard_map/all_to_all | solution.py:57
  482.5 1.2 all_to_all.28
  483.8 8.7 %convert_bitcast_fusion = bf16[16,16,32,180]{3,2,1,0:T(8,128)(2,1)} fusion(bf16[16,180,784,1]{2,1,0,3:T(8,128)(2,1)} %reshape.30, bf16[1,32,16,784]{3,2,1,0:T(8,128)(2,1)S(1)} %all_to_all.28), kind=kOutput, calls=%fused_computation | convolution fusion | flops 2313584640 | bytes 8267776 | tf_op jit(solution)/shard_map/lrc,vdc->lvrd/dot_general | solution.py:58
  492.5 0.0 reduce-scatter.6.cloned.1.call-update
  492.5 0.0 reduce-scatter.8.cloned.1.call-start
  492.5 63.2 %reduce-scatter.6.cloned.1.call-done = bf16[1,16,32,180]{3,2,1,0:T(8,128)(2,1)} async-done(((bf16[16,16,32,180]{3,2,1,0:T(8,128)(2,1)}), bf16[1,16,32,180]{3,2,1,0:T(8,128)(2,1)}) %reduce-scatter.6.cloned.1.call-update) | async-done | bytes 184336 | tf_op jit(solution)/shard_map/reduce_scatter | solution.py:61
  555.8 0.0 reduce-scatter.8.cloned.1.call-update
  555.8 78.6 %reduce-scatter.8.cloned.1.call-done = bf16[1,1,32,180]{3,2,1,0:T(8,128)(2,1)} async-done(((bf16[1,16,32,180]{3,2,1,0:T(8,128)(2,1)}), bf16[1,1,32,180]{3,2,1,0:T(8,128)(2,1)}) %reduce-scatter.8.cloned.1.call-update) | async-done | bytes 11536
  634.4 0.8 fusion.11
  635.2 33.3 %psum.31 = f32[32]{0:T(128)S(1)} all-reduce(f32[32]{0:T(128)S(1)} %fusion.11), channel_id=1, replica_groups=mesh['layer'=16,'vocab'=16] {'vocab'}, use_global_device_ids=true, to_apply=%region_11.0 | all-reduce | flops 32 | bytes 256 | tf_op jit(solution)/shard_map/psum | solution.py:67
  668.5 1.3 convolution_bitcast_fusion
  669.8 3.5 copy.22
  673.3 0.7 fusion.12
  (11 shorter events, 0.0 us)
Async XLA Ops:
  7.2 1.2 copy-start
  7.2 158.0 %all-gather.4.cloned.1.call-start = ((), (), s32[]{:S(2)}) async-start(), calls=%async_computation.5 | async-start | bytes 4210688 | tf_op jit(solution)/shard_map/all_gather | solution.py:42
  45.9 509.9 %reduce-scatter.6.cloned.1.call-start = ((), (), s32[]{:S(2)}) async-start(), calls=%async_computation.4 | async-start | bytes 4456448 | tf_op jit(solution)/shard_map/reduce_scatter | solution.py:61
  223.4 4.5 copy-start.3
  226.5 118.2 %collective-permute-start = (f32[32,12544]{1,0:T(8,128)}, f32[32,12544]{1,0:T(8,128)}, u32[]{:S(2)}, u32[]{:S(2)}) collective-permute-start(f32[32,12544]{1,0:T(8,128)} %squeeze.17), channel_id=1, source_target_pairs={{16,0},{32,16},{48,32},{64,48},{80,64},{96,80},{112,96},{128,112},... | collective-permute-start | bytes 4816904 | tf_op jit(solution)/shard_map/ppermute | solution.py:12
  341.7 3.0 collective-permute-start.1
  492.4 141.9 %copy-start.4 = (f32[180]{0:T(256)S(1)}, f32[180]{0:T(256)}, u32[]{:S(2)}) copy-start(f32[180]{0:T(256)} %param.9) | copy-start | bytes 2164
  492.5 176.0 %copy-start.1 = (bf16[1,32,2880]{2,1,0:T(8,128)(2,1)S(1)}, bf16[1,32,2880]{2,1,0:T(8,128)(2,1)}, u32[]{:S(2)}) copy-start(bf16[1,32,2880]{2,1,0:T(8,128)(2,1)} %param.6) | copy-start | bytes 552964
  492.5 141.9 %reduce-scatter.8.cloned.1.call-start = ((), (), s32[]{:S(2)}) async-start(), calls=%async_computation.6 | async-start | bytes 278528
  669.8 3.5 copy-start.2
Sparse Core Ops, SparseCore 0:
  46.0 119.0 all-gather.3
  492.6 63.1 reduce-scatter.5
  559.2 75.0 reduce-scatter.7
where the time goes:
time: 687 us; the launch traced here: 680 us
  blocking collectives  251 us (37%)
  waiting for transfers between devices  248 us (36%)
  other arithmetic  79.8 us (12%)
  local copies, waits for them, and re-layouts  67.3 us (10%)
  matrix products  18.3 us (3%)
  between operations  13.9 us (2%)
    all_gather x1, waiting for transfers between devices, on_device(): lax.all_gather(normed[None], ('layer', 'vocab'), axis=0, tiled=True)  104 us
    unnamed x4, waiting for transfers between devices  78.6 us
    unnamed x1, other arithmetic  70.2 us
    reduce_scatter x1, waiting for transfers between devices, on_device(): lax.psum_scatter(partial_value.astype(jnp.bfloat16), 'layer', scatter_dim...  63.2 us
    all_to_all x1, blocking collectives, on_device(): lax.all_to_all(logits, 'layer', split_axis=0, concat_axis=2, tiled=True)[0]  49 us
    all_gather x1, blocking collectives, on_device(): lax.all_gather(final_logits, 'layer', axis=1, tiled=True)  36.1 us
    psum x1, blocking collectives, stats_narrow(): lax.psum((jnp.sum(jnp.exp(final_f32 - row_top[:, None]), axis=1), lens_to...  35 us
    psum x1, blocking collectives, on_device(): squares = lax.psum(jnp.sum(lens_out * lens_out, axis=1), 'vocab')  34.6 us
  transfers between devices with their start and end apart: 5, of which 4 were waited for; matrix products, arithmetic and copies ran while one was open for 4% of the time, Pallas kernels for 0%

commit v1 on v0

v1 whole, which is shorter than its diff:
```python
import functools

import jax
import jax.numpy as jnp
from jax import lax
from jax.experimental import pallas as pl
from jax.experimental.pallas import tpu as pltpu
from jax.sharding import PartitionSpec as P

MESH = pl.DeviceIdType.MESH
F32, BF16 = jnp.float32, jnp.bfloat16
EPS = 1e-05
D, ROWS, OWN, SHARD = 2880, 32, 180, 784
WIN, HALF, QUART = 192, 96, 48
STEP = 176
QUAD = 4 * OWN
TILE = 112


def split3(value):
    high = value.astype(BF16).astype(F32)
    rest = value - high
    mid = rest.astype(BF16).astype(F32)
    return high, mid, (rest - mid).astype(BF16).astype(F32)


def kernel(hid_h, trans_h, bias_h, gain_h, un_h, fin_h, out_ref,
           hid, hpad, trans, bias, gain, un, unt, fin, fint,
           lens, zbuf, nt, dense, stat, logits, inv, grad, gt, core_in,
           zx, zz, ra, rb, rc, rd, q, qown, re, rf, rg, rh, fz32, fz16, fzr,
           local, gz_s, gz_r, gx_s, gx_r, gc_s, gc_r, zx_s, zx_r, zz_s, zz_r,
           ce_s, ce_r, rs_s, rs_r, fz_s, fz_r):
    layer, voc = lax.axis_index("layer"), lax.axis_index("vocab")
    z, c = layer // 2, layer % 2
    x, y = voc // 4, voc % 4
    other = 1 - c
    sibling = (z * 2 + other, voc)

    def remote(src, dst, send, recv, device):
        return pltpu.make_async_remote_copy(
            src_ref=src, dst_ref=dst, send_sem=send, recv_sem=recv,
            device_id=device, device_id_type=MESH)

    barrier = pltpu.get_barrier_semaphore()

    def greet(k, _):
        pl.semaphore_signal(barrier, inc=1, device_id=(layer, (voc + k) % 16), device_id_type=MESH)
        pl.semaphore_signal(barrier, inc=1, device_id=((layer + k) % 16, voc), device_id_type=MESH)
        return 0

    lax.fori_loop(1, 16, greet, 0)

    loads = [pltpu.make_async_copy(a, b, local.at[i]) for i, (a, b) in enumerate(
        [(hid_h, hid), (trans_h, trans), (bias_h, bias), (gain_h, gain), (fin_h, fin), (un_h, un)])]
    for load in loads:
        load.start()
    for load in loads[:5]:
        load.wait()

    hpad[...] = jnp.zeros_like(hpad)
    hpad[:, 0:D] = hid[...].astype(F32)
    first = voc * OWN
    tile = first // 128
    near = hpad[:, pl.ds(pl.multiple_of(tile * 128, 128), 384)]
    own = pltpu.roll(near, (384 - (first - tile * 128)) % 384, axis=1)[:, 0:OWN]
    lens_out = own + lax.dot_general(hid[...], trans[...], (((1,), (1,)), ((), ())),
                                     preferred_element_type=F32) + bias[...]
    shift = y * 4
    base = jnp.where(y < 2, 184, 0)
    lens[...] = jnp.zeros_like(lens)
    lens[:, 0:OWN] = lens_out * gain[...]
    pay = pltpu.roll(lens[...], shift, axis=1)
    lens[:, 0:OWN] = lens_out
    squares = jnp.sum(lens_out * lens_out, axis=1, keepdims=True)
    final = fin[...].astype(F32)
    top = jnp.max(final, axis=1, keepdims=True)
    total = jnp.sum(jnp.exp(final - top), axis=1, keepdims=True)
    lane = lax.broadcasted_iota(jnp.int32, (ROWS, 256), 1)
    for k, value in enumerate((*split3(squares), top, *split3(total))):
        pay = jnp.where(lane == base + k, value, pay)
    zbuf[z] = pay.astype(BF16)

    pl.semaphore_wait(barrier, 30)

    def z_copy(k):
        return remote(zbuf.at[z], zbuf.at[z], gz_s.at[k], gz_r.at[k], (((z + k) % 8) * 2 + c, voc))

    for k in range(1, 8):
        z_copy(k).start()

    fint[...] = jnp.concatenate([final] * 4, axis=0).T
    loads[5].wait()
    eye = (lax.broadcasted_iota(jnp.int32, (256, 256), 0)
           == lax.broadcasted_iota(jnp.int32, (256, 256), 1)).astype(BF16)

    def turn(i, _):
        at = pl.multiple_of(i * 256, 256)
        unt[pl.ds(at, 256), :] = lax.dot_general(
            eye, un[:, pl.ds(at, 256)], (((1,), (1,)), ((), ())),
            preferred_element_type=F32).astype(BF16)
        return 0

    lax.fori_loop(0, 11, turn, 0)
    unt[2816:D, :] = lax.dot_general(
        eye[0:64, 0:64], un[:, 2816:D], (((1,), (1,)), ((), ())),
        preferred_element_type=F32).astype(BF16)

    for k in range(1, 8):
        z_copy(k).wait_recv()
    turned = zbuf[...].astype(F32).reshape(256, 256).T.astype(BF16)
    nt[c, 0, x, y] = turned[0:HALF]
    nt[c, 1, y, x] = turned[HALF:WIN]

    def place(h, f, s):
        return (layer, f * 4 + s) if h == 0 else (layer, s * 4 + f)

    ring = []
    for h, (f, s) in enumerate(((x, y), (y, x))):
        ring.append((f, (f + 3) % 4, (f + 1) % 4, (f + 2) % 4, s, (s + 3) % 4, (s + 1) % 4, (s + 2) % 4))

    def along_f(h, k):
        f, fm, fp, fo, s, sm, sp, so = ring[h]
        src = (nt.at[c, h, f, s], nt.at[c, h, f, s],
               nt.at[c, h, fm, s, pl.ds(0, QUART)], nt.at[c, h, fp, s, pl.ds(QUART, QUART)])[k]
        land = (nt.at[c, h, fm, s], nt.at[c, h, fp, s],
                nt.at[c, h, fo, s, pl.ds(0, QUART)], nt.at[c, h, fo, s, pl.ds(QUART, QUART)])[k]
        to = (fp, fm, fp, fm)[k]
        return src, land, gx_s.at[h, k], gx_r.at[h, k], place(h, to, s)

    def along_s(h, j, k):
        f, fm, fp, fo, s, sm, sp, so = ring[h]
        g = (f, fm, fp, fo)[j]
        n = 4 + 4 * j + k
        src = (nt.at[c, h, g, s], nt.at[c, h, g, s],
               nt.at[c, h, g, sm, pl.ds(0, QUART)], nt.at[c, h, g, sp, pl.ds(QUART, QUART)])[k]
        land = (nt.at[c, h, g, sm], nt.at[c, h, g, sp],
                nt.at[c, h, g, so, pl.ds(0, QUART)], nt.at[c, h, g, so, pl.ds(QUART, QUART)])[k]
        to = (sp, sm, sp, sm)[k]
        return src, land, gx_s.at[h, n], gx_r.at[h, n], place(h, f, to)

    def share(h, j):
        f, fm, fp, fo = ring[h][:4]
        g = (f, fm, fp, fo)[j]
        src, land = nt.at[c, h, g], nt.at[other, h, g]
        n = 4 * h + j
        return src, land, gc_s.at[n], gc_r.at[n], sibling

    def go(copy):
        remote(copy[0], copy[0], *copy[2:]).start()

    def come(copy):
        remote(copy[1], copy[1], *copy[2:]).wait_recv()

    def gone(copy):
        remote(copy[0], copy[0], *copy[2:]).wait_send()

    both = (0, 1)
    for h in both:
        for k in (0, 1):
            go(along_f(h, k))
    for h in both:
        for k in (0, 1):
            go(along_s(h, 0, k))
    for h in both:
        for k in (0, 1):
            come(along_f(h, k))
            go(along_f(h, 2 + k))
    for h in both:
        for j in (1, 2):
            for k in (0, 1):
                go(along_s(h, j, k))
    for h in both:
        for k in (0, 1):
            come(along_s(h, 0, k))
            go(along_s(h, 0, 2 + k))
    for h in both:
        for k in (2, 3):
            come(along_f(h, k))
        for k in (0, 1):
            go(along_s(h, 3, k))
    for j in (1, 2):
        for h in both:
            for k in (0, 1):
                come(along_s(h, j, k))
                go(along_s(h, j, 2 + k))
    for h in both:
        for k in (2, 3):
            come(along_s(h, 0, k))
        go(share(h, 0))
    for h in both:
        for k in (0, 1):
            come(along_s(h, 3, k))
            go(along_s(h, 3, 2 + k))
    for j in (1, 2, 3):
        for h in both:
            for k in (2, 3):
                come(along_s(h, j, k))
            go(share(h, j))
    for h in both:
        for j in range(4):
            come(share(h, j))

    row16 = lax.broadcasted_iota(jnp.int32, (16, 256), 0)

    def join(i, _):
        for p in (0, 1):
            for w in range(4):
                at = pl.multiple_of(i * QUAD, 16) + STEP * w
                head = nt[p, 0, i, w, 0:16]
                if w:
                    tail = nt[p, 1, w - 1, i, 80:96]
                    head = jnp.where(row16 < 4 * w, tail.astype(F32), head.astype(F32)).astype(BF16)
                dense[p, pl.ds(at, 16)] = head
                dense[p, pl.ds(at + 16, 80)] = nt[p, 0, i, w, 16:96]
                if w < 3:
                    dense[p, pl.ds(at + 96, 80)] = nt[p, 1, w, i, 0:80]
                else:
                    dense[p, pl.ds(at + 96, 96)] = nt[p, 1, w, i]
                piece = nt[p, 1, w, i, 80:96].astype(F32)[8:16] if w < 2 else nt[p, 0, i, w, 0:16].astype(F32)[0:8]
                stat[p, i * 4 + w] = piece
        return 0

    lax.fori_loop(0, 4, join, 0)

    tops = []
    for p in (0, 1):
        sums = jnp.sum(stat[p], axis=0)
        inv[p] = jnp.broadcast_to(
            lax.rsqrt((sums[0:1] + sums[1:2] + sums[2:3]) / D + EPS), (8, 256))
        tops.append(jnp.max(stat[p], axis=0)[3:4])
    most = jnp.maximum(tops[0], tops[1])
    most = jnp.broadcast_to(jnp.maximum(most[:, 0:128], most[:, 128:256]), (8, 128))
    for turn_by in (32, 64):
        most = jnp.maximum(most, pltpu.roll(most, turn_by, axis=1))
    wide = jnp.concatenate([most, most], axis=1)[0:1]
    sums = jnp.zeros((1, 256), F32)
    for p in (0, 1):
        scaled = jnp.exp(stat[p, :, 3:4, :] - wide[None])
        part = (stat[p, :, 4:5, :] + stat[p, :, 5:6, :] + stat[p, :, 6:7, :]) * scaled
        sums += jnp.sum(part, axis=0)
    sums = jnp.broadcast_to(sums[:, 0:128] + sums[:, 128:256], (8, 128))
    for turn_by in (32, 64):
        sums += pltpu.roll(sums, turn_by, axis=1)
    final_lse = (most + jnp.log(sums))[0:1]

    for n, (at, depth) in enumerate(((0, 768), (768, 768), (1536, 768), (2304, 576))):
        for p in (0, 1):
            part = jnp.dot(un[:, at:at + depth], dense[p, at:at + depth], preferred_element_type=F32)
            if n:
                logits[p] += part
            else:
                logits[p] = part

    def fold(value):
        return jnp.sum(value.reshape(TILE // 8, 8, 256), axis=0)

    def totals(i, carry):
        at = pl.multiple_of(i * TILE, TILE)
        out = []
        for p in (0, 1):
            value = logits[p, pl.ds(at, TILE)] * inv[p, 0:1]
            logits[p, pl.ds(at, TILE)] = value
            out.append(carry[p] + fold(jnp.exp(value)))
        return tuple(out)

    zero = jnp.zeros((8, 256), F32)
    sums = lax.fori_loop(0, SHARD // TILE, totals, (zero, zero))
    sums = [jnp.sum(value, axis=0, keepdims=True) for value in sums]

    zx[voc] = jnp.concatenate(
        [sums[0][:, 0:128], sums[0][:, 128:256], sums[1][:, 0:128], sums[1][:, 128:256],
         jnp.zeros((4, 128), F32)], axis=0)

    def zx_copy(k):
        return remote(zx.at[voc], zx.at[voc], zx_s.at[k], zx_r.at[k], (layer, (voc + k) % 16))

    def zz_copy(k):
        return remote(zz.at[layer], zz.at[layer], zz_s.at[k], zz_r.at[k], ((layer + k) % 16, voc))

    def each(lo, hi, act):
        def body(k, _):
            act(k)
            return 0
        lax.fori_loop(lo, hi, body, 0)

    each(1, 16, lambda k: zx_copy(k).start())
    each(1, 16, lambda k: zx_copy(k).wait_recv())
    zz[layer] = jnp.sum(zx[...], axis=0)
    each(1, 16, lambda k: zz_copy(k).start())
    each(1, 16, lambda k: zz_copy(k).wait_recv())
    lse = jnp.log(jnp.sum(zz[...], axis=0)[0:4])
    lse = [jnp.concatenate([lse[2 * p:2 * p + 1], lse[2 * p + 1:2 * p + 2]], axis=1) for p in (0, 1)]

    last = lax.broadcasted_iota(jnp.int32, (1, 256), 1) < 224

    def slopes(i, carry):
        at = pl.multiple_of(i * TILE, TILE)
        rows = pl.ds(at, TILE)
        x0, x1 = logits[0, rows], logits[1, rows]
        p0, p1 = jnp.exp(x0 - lse[0]), jnp.exp(x1 - lse[1])
        pf = jnp.exp(fint[rows] - final_lse)
        pf = jnp.concatenate([pf, pf], axis=1)
        after = pltpu.roll(p0, 224, axis=1)
        g0 = (p0 - pf) + (p0 - p1)
        g1 = (p1 - pf) + jnp.where(last, p1 - after, 0.0)
        grad[0, rows] = g0.astype(BF16)
        grad[1, rows] = g1.astype(BF16)
        return carry[0] + fold(g0 * x0), carry[1] + fold(g1 * x1)

    proj = lax.fori_loop(0, SHARD // TILE, slopes, (zero, zero))
    tagged = []
    row8 = lax.broadcasted_iota(jnp.int32, (8, 256), 0)
    for p in (0, 1):
        value = jnp.sum(proj[p], axis=0, keepdims=True)
        high = value.astype(BF16).astype(F32)
        tagged.append(jnp.where(row8 == 0, high, value - high))

    def product(p, tag, i):
        rows = pl.ds(pl.multiple_of(i * QUAD, 16), QUAD)
        value = jnp.dot(unt[rows, :], grad[p], preferred_element_type=F32)
        for w in range(4):
            one, two = value[STEP * w:STEP * w + HALF], value[STEP * w + HALF:STEP * w + WIN]
            if w < 2:
                two = jnp.concatenate([two[0:88], jnp.where(row8 < 2, tag, two[88:96])], axis=0)
            else:
                one = jnp.concatenate([jnp.where(row8 < 2, tag, one[0:8]), one[8:96]], axis=0)
            gt[p, 0, i, w] = one.astype(BF16)
            gt[p, 1, w, i] = two.astype(BF16)

    def cross(i, h):
        src = gt.at[other, 0, i] if h == 0 else gt.at[other, 1, :, i]
        land = core_in.at[0, i] if h == 0 else core_in.at[1, :, i]
        n = 4 * h + i
        return remote(src, land, ce_s.at[n], ce_r.at[n], sibling)

    tag_other = jnp.where(c == 0, tagged[1], tagged[0])
    tag_own = jnp.where(c == 0, tagged[0], tagged[1])

    def away(i, _):
        product(other, tag_other, i)
        cross(i, 0).start()
        cross(i, 1).start()
        return 0

    lax.fori_loop(0, 4, away, 0)

    def home(i, _):
        product(c, tag_own, i)
        return 0

    lax.fori_loop(0, 4, home, 0)

    def merge(i, _):
        for h in (0, 1):
            cross(i, h).wait_recv()
        for w in range(4):
            gt[c, 0, i, w] = (gt[c, 0, i, w].astype(F32) + core_in[0, i, w].astype(F32)).astype(BF16)
            gt[c, 1, w, i] = (gt[c, 1, w, i].astype(F32) + core_in[1, w, i].astype(F32)).astype(BF16)
        return 0

    lax.fori_loop(0, 4, merge, 0)

    def add(ref, at, got):
        ref[at] = (ref[at].astype(F32) + got.astype(F32)).astype(BF16)

    def scatter(h, k):
        f, fm, fp, fo, s, sm, sp, so = ring[h]
        lo, hi = pl.ds(0, QUART), pl.ds(QUART, QUART)
        src = (gt.at[c, h, :, so, lo], gt.at[c, h, :, so, hi], gt.at[c, h, :, sp], gt.at[c, h, :, sm],
               q.at[h, fo, lo], q.at[h, fo, hi], q.at[h, fp], q.at[h, fm])[k]
        land = (ra.at[h], rb.at[h], rc.at[h], rd.at[h], re.at[h], rf.at[h], rg.at[h], rh.at[h])[k]
        to = place(h, f, (sp, sm)[k % 2]) if k < 4 else place(h, (fp, fm)[k % 2], s)
        return remote(src, land, rs_s.at[h, k], rs_r.at[h, k], to)

    for h in both:
        scatter(h, 0).start()
        scatter(h, 1).start()
    for h in both:
        f, fm, fp, fo, s, sm, sp, so = ring[h]
        scatter(h, 0).wait_recv()
        for g in range(4):
            add(gt, (c, h, g, sp, pl.ds(0, QUART)), ra[h, g])
        scatter(h, 2).start()
        scatter(h, 1).wait_recv()
        for g in range(4):
            add(gt, (c, h, g, sm, pl.ds(QUART, QUART)), rb[h, g])
        scatter(h, 3).start()
    for h in both:
        f, fm, fp, fo, s, sm, sp, so = ring[h]
        scatter(h, 2).wait_recv()
        scatter(h, 3).wait_recv()
        for g in range(4):
            q[h, g] = (gt[c, h, g, s].astype(F32) + rc[h, g].astype(F32) + rd[h, g].astype(F32)).astype(BF16)
        qown[h] = gt[c, h, f, s].astype(F32) + rc[h, f].astype(F32) + rd[h, f].astype(F32)
        scatter(h, 4).start()
        scatter(h, 5).start()
    for h in both:
        f, fm, fp, fo, s, sm, sp, so = ring[h]
        scatter(h, 4).wait_recv()
        add(q, (h, fp, pl.ds(0, QUART)), re[h])
        scatter(h, 6).start()
        scatter(h, 5).wait_recv()
        add(q, (h, fm, pl.ds(QUART, QUART)), rf[h])
        scatter(h, 7).start()
    whole = []
    for h in both:
        scatter(h, 6).wait_recv()
        scatter(h, 7).wait_recv()
        whole.append(qown[h] + rg[h].astype(F32) + rh[h].astype(F32))

    own_inv = jnp.where(c == 0, inv[0], inv[1])
    full = jnp.concatenate([*whole, own_inv, jnp.zeros((56, 256), F32)], axis=0).T
    fz32[...] = full.reshape(8, ROWS, 256)
    fz16[...] = fz32[...].astype(BF16)

    def fz_copy(k):
        to = (z + k) % 8
        return remote(fz16.at[to], fzr.at[k], fz_s.at[k], fz_r.at[k], (to * 2 + c, voc))

    for k in range(1, 8):
        fz_copy(k).start()
    grown = fz32[z]
    inv_col = grown[:, WIN:WIN + 1]
    for k in range(1, 8):
        fz_copy(k).wait_recv()
        grown += fzr[k].astype(F32)
    along = jnp.sum(jnp.where((lane == base) | (lane == base + 1), grown, 0.0), axis=1, keepdims=True)
    grown = pltpu.roll(grown, (256 - shift) % 256, axis=1)[:, 0:OWN]
    out_ref[...] = inv_col * gain[...] * grown - lens[:, 0:OWN] * (inv_col * inv_col * along / D)

    for k in range(1, 8):
        z_copy(k).wait_send()
        fz_copy(k).wait_send()
    for h in both:
        for k in range(4):
            gone(along_f(h, k))
            for j in range(4):
                gone(along_s(h, j, k))
            gone(share(h, k))
            cross(k, h).wait_send()
        for k in range(8):
            scatter(h, k).wait_send()
    each(1, 16, lambda k: zx_copy(k).wait_send())
    each(1, 16, lambda k: zz_copy(k).wait_send())


def weights(hid_ref, go_ref, out_ref, bias_ref):
    turned = go_ref[...].T
    bias_ref[...] = jnp.sum(go_ref[...], axis=0, keepdims=True)
    value = jnp.dot(turned.astype(BF16), hid_ref[...], preferred_element_type=F32)
    out_ref[...] = value.reshape(out_ref.shape)


def on_device(hidden, translator, bias, gain, unembed, final_logits):
    vmem, sem = pltpu.VMEM, pltpu.SemaphoreType.DMA
    anywhere = pl.BlockSpec(memory_space=pl.ANY)
    inside = pl.BlockSpec(memory_space=pltpu.VMEM)
    grad_out = pl.pallas_call(
        kernel,
        out_shape=jax.ShapeDtypeStruct((ROWS, OWN), F32),
        in_specs=[anywhere] * 6,
        out_specs=inside,
        scratch_shapes=[
            vmem((ROWS, D), BF16), vmem((ROWS, 3072), F32), vmem((OWN, D), BF16),
            vmem((1, OWN), F32), vmem((1, OWN), F32),
            vmem((SHARD, D), BF16), vmem((D, SHARD), BF16),
            vmem((ROWS, SHARD), BF16), vmem((SHARD, 128), F32),
            vmem((ROWS, 256), F32), vmem((8, ROWS, 256), BF16),
            vmem((2, 2, 4, 4, HALF, 256), BF16), vmem((2, D, 256), BF16),
            vmem((2, 16, 8, 256), F32), vmem((2, SHARD, 256), F32), vmem((2, 8, 256), F32),
            vmem((2, SHARD, 256), BF16), vmem((2, 2, 4, 4, HALF, 256), BF16),
            vmem((2, 4, 4, HALF, 256), BF16),
            vmem((16, 8, 128), F32), vmem((16, 8, 128), F32),
            vmem((2, 4, QUART, 256), BF16), vmem((2, 4, QUART, 256), BF16),
            vmem((2, 4, HALF, 256), BF16), vmem((2, 4, HALF, 256), BF16),
            vmem((2, 4, HALF, 256), BF16), vmem((2, HALF, 256), F32),
            vmem((2, QUART, 256), BF16), vmem((2, QUART, 256), BF16),
            vmem((2, HALF, 256), BF16), vmem((2, HALF, 256), BF16),
            vmem((8, ROWS, 256), F32), vmem((8, ROWS, 256), BF16), vmem((8, ROWS, 256), BF16),
            sem((6,)), sem((8,)), sem((8,)), sem((2, 20)), sem((2, 20)), sem((8,)), sem((8,)),
            sem((16,)), sem((16,)), sem((16,)), sem((16,)),
            sem((8,)), sem((8,)), sem((2, 8)), sem((2, 8)), sem((8,)), sem((8,)),
        ],
        compiler_params=pltpu.CompilerParams(
            collective_id=0, has_side_effects=True, vmem_limit_bytes=58 * 1024 * 1024),
    )(hidden[0], translator[0].T, bias, gain.reshape(1, OWN), unembed.T, final_logits)
    grad_translator, grad_bias = pl.pallas_call(
        weights,
        out_shape=(jax.ShapeDtypeStruct((OWN, 1, D), F32), jax.ShapeDtypeStruct((1, OWN), F32)),
        in_specs=[inside, inside],
        out_specs=(inside, inside),
        compiler_params=pltpu.CompilerParams(vmem_limit_bytes=32 * 1024 * 1024),
    )(hidden[0], grad_out)
    return jnp.transpose(grad_translator, (1, 2, 0)), grad_bias


def solution(mesh):
    placed = (
        P("layer", None, None),
        P("layer", None, "vocab"),
        P("layer", "vocab"),
        P("vocab"),
        P(None, ("layer", "vocab")),
        P(None, ("layer", "vocab")),
    )
    return jax.shard_map(
        on_device,
        mesh=mesh,
        in_specs=placed,
        out_specs=(P("layer", None, "vocab"), P("layer", "vocab")),
        check_vma=False,
    )
```

time: 687 us -> 79.5 us (0.12)
  blocking collectives: 251 us -> 0 us
  waiting for transfers between devices: 248 us -> 0 us
  other arithmetic: 79.8 us -> 0 us
  Pallas kernels: 0 us -> 78 us
  local copies, waits for them, and re-layouts: 67.3 us -> 0.76 us
  matrix products: 18.3 us -> 0 us
  between operations: 13.9 us -> 0.66 us
    all_gather x1 -> x0, waiting for transfers between devices: 104 us -> none  [on_device(): lax.all_gather(normed[None], ('layer', 'vocab'), axis=0, tiled=True)]
    psum x3 -> x0, blocking collectives: 103 us -> none  [the longest x1 35 us: stats_narrow(): lax.psum((jnp.sum(jnp.exp(final_f32 - row_top[:, None]), axis=1), lens_to...]
    unnamed x4 -> x0, waiting for transfers between devices: 78.6 us -> none
    all_to_all x2 -> x0, blocking collectives: 78.2 us -> none  [the longest x1 49 us: on_device(): lax.all_to_all(logits, 'layer', split_axis=0, concat_axis=2, tiled=True)[0]]
    pallas_call x0 -> x2, Pallas kernels: none -> 78 us  [the longest x1 76 us: on_device(): pl.pallas_call(kernel, out_shape=jax.ShapeDtypeStruct((ROWS, OWN), F32),...]
    unnamed x1 -> x0, other arithmetic: 70.2 us -> none
    reduce_scatter x1 -> x0, waiting for transfers between devices: 63.2 us -> none  [on_device(): lax.psum_scatter(partial_value.astype(jnp.bfloat16), 'layer', scatter_dim...]
    all_gather x1 -> x0, blocking collectives: 36.1 us -> none  [on_device(): lax.all_gather(final_logits, 'layer', axis=1, tiled=True)]
  transfers between devices with their start and end apart: 5 -> 0, of which waited for: 4 -> 0; matrix products, arithmetic and copies ran while one was open for 4% -> 0% of each run, Pallas kernels for 0% -> 0%
where the time goes in v1:
time: 79.5 us; the launch traced here: 79.4 us
  Pallas kernels  78 us (98%)
    pallas_call x1, Pallas kernels, on_device(): pl.pallas_call(kernel, out_shape=jax.ShapeDtypeStruct((ROWS, OWN), F32),...  76 us
    pallas_call x1, Pallas kernels, on_device(): pl.pallas_call(weights, out_shape=(jax.ShapeDtypeStruct((OWN, 1, D), F32)...  1.97 us

profile of v1, /device:TPU:2, one launch (start us, length us, event | category | flops | bytes accessed | tf_op | source)
XLA Modules:
  0.0 79.4 jit_solution(13747796289284803615)
XLA Ops:
  0.6 0.0 copy-start
  0.6 76.0 %shard_map.77.go_ref = f32[32,180]{1,0:T(8,128)} custom-call(bf16[32,2880]{1,0:T(8,128)(2,1)} %bitcast.7, bf16[180,2880]{1,0:T(8,128)(2,1)} %bitcast.10, f32[1,180]{1,0:T(1,128)} %bias_h.1, f32[1,180]{1,0:T(1,128)} %bitcast.11, bf16[784,2880]{1,0:T(8,128)(2,1)} %bitcast.9, bf16[32,784]{1,0:T(8,128)(2,1)} %fin_h.1), custom_call_target="tpu_custom_call" | custom-call | tf_op jit(solution)/shard_map/pallas_call | solution.py:458
  76.6 0.0 copy-done
  76.6 0.0 copy-start.1
  76.7 0.7 copy-done.1
  77.4 2.0 %shard_map.78 = (f32[180,1,2880]{2,1,0:T(1,128)}, f32[1,180]{1,0:T(1,128)}) custom-call(bf16[32,2880]{1,0:T(8,128)(2,1)S(1)} %bitcast.8, f32[32,180]{1,0:T(8,128)S(1)} %copy-done.1), custom_call_target="tpu_custom_call" | custom-call | tf_op jit(solution)/shard_map/pallas_call | solution.py:487
Async XLA Ops:
  0.6 76.0 %copy-start = (bf16[1,32,2880]{2,1,0:T(8,128)(2,1)S(1)}, bf16[1,32,2880]{2,1,0:T(8,128)(2,1)}, u32[]{:S(2)}) copy-start(bf16[1,32,2880]{2,1,0:T(8,128)(2,1)} %param.6) | copy-start | bytes 552964
  76.6 0.8 copy-start.1

commit v2 on v0

v2 whole, which is shorter than its diff:
```python
import functools

import jax
import jax.numpy as jnp
from jax import lax
from jax.experimental import pallas as pl
from jax.experimental.pallas import tpu as pltpu
from jax.sharding import PartitionSpec as P

MESH = pl.DeviceIdType.MESH
F32, BF16 = jnp.float32, jnp.bfloat16
EPS = 1e-05
D, ROWS, OWN, SHARD = 2880, 32, 180, 784
WIN, HALF = 192, 96
STEP = 176
QUAD = 4 * OWN
TILE = 112
NEAR = (1, 3, 2)
FAR = (2, 1, 3)


def split3(value):
    high = value.astype(BF16).astype(F32)
    rest = value - high
    mid = rest.astype(BF16).astype(F32)
    return high, mid, (rest - mid).astype(BF16).astype(F32)


def kernel(hid_h, trans_h, bias_h, gain_h, un_h, fin_h, out_ref,
           hid, hpad, trans, bias, gain, un, unt, fin, fint,
           lens, zbuf, nt, dense, stat, logits, inv, grad, gt, core_in,
           zx, zz, sin, q, qown, fzin, fz32, fz16, fzr,
           local, gz_s, gz_r, gf_s, gf_r, gs_s, gs_r, gc_s, gc_r, zx_s, zx_r, zz_s, zz_r,
           ce_s, ce_r, ss_s, ss_r, sf_s, sf_r, fz_s, fz_r):
    layer, voc = lax.axis_index("layer"), lax.axis_index("vocab")
    z, c = layer // 2, layer % 2
    x, y = voc // 4, voc % 4
    other = 1 - c
    sibling = (z * 2 + other, voc)

    def remote(src, dst, send, recv, device):
        return pltpu.make_async_remote_copy(
            src_ref=src, dst_ref=dst, send_sem=send, recv_sem=recv,
            device_id=device, device_id_type=MESH)

    def begin(copy, *at):
        copy(*at).start()

    def sent(ref, semaphore):
        remote(ref, ref, semaphore, semaphore, sibling).wait_send()

    def landed(ref, semaphore):
        remote(ref, ref, semaphore, semaphore, sibling).wait_recv()

    def each(lo, hi, act):
        def body(k, _):
            act(k)
            return 0
        lax.fori_loop(lo, hi, body, 0)

    barrier = pltpu.get_barrier_semaphore()

    def greet(k):
        pl.semaphore_signal(barrier, inc=1, device_id=((layer + k) % 16, voc), device_id_type=MESH)
        pl.semaphore_signal(barrier, inc=1, device_id=(layer, (voc + k) % 16), device_id_type=MESH)

    loads = [pltpu.make_async_copy(a, b, local.at[i]) for i, (a, b) in enumerate(
        [(trans_h, trans), (hid_h, hid), (bias_h, bias), (gain_h, gain), (fin_h, fin)])]
    parts = [pltpu.make_async_copy(un_h.at[pl.ds(i * TILE, TILE)], un.at[pl.ds(i * TILE, TILE)], local.at[5])
             for i in range(SHARD // TILE)]
    for load in loads:
        load.start()
    each(1, 16, greet)

    loads[4].wait()
    final = fin[...].astype(F32)
    top = jnp.max(final, axis=1, keepdims=True)
    total = jnp.sum(jnp.exp(final - top), axis=1, keepdims=True)

    for load in loads[:4]:
        load.wait()
    hpad[:, 2688:3072] = jnp.zeros((ROWS, 384), F32)
    hpad[:, 0:D] = hid[...].astype(F32)
    first = voc * OWN
    tile = first // 128
    near = hpad[:, pl.ds(pl.multiple_of(tile * 128, 128), 384)]
    own = pltpu.roll(near, (384 - (first - tile * 128)) % 384, axis=1)[:, 0:OWN]
    lens_out = own + lax.dot_general(hid[...], trans[...], (((1,), (1,)), ((), ())),
                                     preferred_element_type=F32) + bias[...]
    shift = y * 4
    base = jnp.where(y < 2, 184, 0)
    lens[...] = jnp.zeros_like(lens)
    lens[:, 0:OWN] = lens_out * gain[...]
    pay = pltpu.roll(lens[...], shift, axis=1)
    lens[:, 0:OWN] = lens_out
    squares = jnp.sum(lens_out * lens_out, axis=1, keepdims=True)
    lane = lax.broadcasted_iota(jnp.int32, (ROWS, 256), 1)
    for k, value in enumerate((*split3(squares), top, *split3(total))):
        pay = jnp.where(lane == base + k, value, pay)
    zbuf[z] = pay.astype(BF16)

    pl.semaphore_wait(barrier, 30)

    def z_send(k):
        return remote(zbuf.at[z], zbuf.at[z], gz_s.at[0], gz_r.at[z // 4], (((z + k) % 8) * 2 + c, voc))

    def z_come(g):
        @pl.when(z // 4 == g)
        def _():
            landed(zbuf.at[pl.ds(4 * g, 3)], gz_r.at[g])

        @pl.when(z // 4 != g)
        def _():
            landed(zbuf.at[pl.ds(4 * g, 4)], gz_r.at[g])

    for k in (4, 3, 5, 2, 6, 1, 7):
        begin(z_send, k)
    for part in parts:
        part.start()

    axes = ((x, y), (y, x))

    def place(h, f, s):
        return (layer, f * 4 + s) if h == 0 else (layer, s * 4 + f)

    def f_send(g, h, k):
        f, s = axes[h]
        src = nt.at[c, g, h, f, s]
        return remote(src, src, gf_s.at[0], gf_r.at[g, h, k - 1], place(h, (f + k) % 4, s))

    def f_come(g, h, k):
        f, s = axes[h]
        land = nt.at[c, g, h, (f + 4 - k) % 4, s]
        landed(land, gf_r.at[g, h, k - 1])

    def s_send(g, h, j, k):
        f, s = axes[h]
        src = nt.at[c, g, h, (f + 4 - j) % 4, s]
        return remote(src, src, gs_s.at[0], gs_r.at[g, h, j], place(h, f, (s + k) % 4))

    def s_come(g, h, j):
        f, s = axes[h]
        landed(nt.at[c, g, h, (f + 4 - j) % 4, pl.ds(0, 3)], gs_r.at[g, h, j])

    def share(g, h, j):
        f, s = axes[h]
        src = nt.at[c, g, h, (f + 4 - j) % 4]
        return remote(src, src, gc_s.at[0], gc_r.at[g], sibling)

    def share_come(g):
        landed(nt.at[other, g], gc_r.at[g])

    both = (0, 1)

    def gather_own(g):
        z_come(g)
        turned = zbuf[4 * g:4 * g + 4].astype(F32).reshape(128, 256).T.astype(BF16)
        nt[c, g, 0, x, y] = turned[0:HALF]
        nt[c, g, 1, y, x] = turned[HALF:WIN]
        for k in FAR:
            for h in both:
                begin(f_send, g, h, k)
        for k in FAR:
            for h in both:
                begin(s_send, g, h, 0, k)

    def gather_on(g):
        for j in NEAR:
            for h in both:
                f_come(g, h, j)
                for k in FAR:
                    begin(s_send, g, h, j, k)

    def gather_end(g):
        for j in (0, *NEAR):
            for h in both:
                s_come(g, h, j)
                begin(share, g, h, j)

    row16 = lax.broadcasted_iota(jnp.int32, (16, 128), 0)

    def join(g):
        def body(i):
            for p in both:
                cols = slice(128 * p, 128 * p + 128)
                for w in range(4):
                    at = pl.multiple_of(i * QUAD, 16) + STEP * w
                    head = nt[p, g, 0, i, w, 0:16]
                    if w:
                        tail = nt[p, g, 1, w - 1, i, 80:96]
                        head = jnp.where(row16 < 4 * w, tail.astype(F32), head.astype(F32)).astype(BF16)
                    dense[g, pl.ds(at, 16), cols] = head
                    dense[g, pl.ds(at + 16, 80), cols] = nt[p, g, 0, i, w, 16:96]
                    if w < 3:
                        dense[g, pl.ds(at + 96, 80), cols] = nt[p, g, 1, w, i, 0:80]
                    else:
                        dense[g, pl.ds(at + 96, 96), cols] = nt[p, g, 1, w, i]
                    if w < 2:
                        piece = nt[p, g, 1, w, i, 80:96].astype(F32)[8:16]
                    else:
                        piece = nt[p, g, 0, i, w, 0:16].astype(F32)[0:8]
                    stat[g, i * 4 + w, :, cols] = piece

        each(0, 4, body)
        sums = jnp.sum(stat[g], axis=0)
        inv[g] = jnp.broadcast_to(lax.rsqrt((sums[0:1] + sums[1:2] + sums[2:3]) / D + EPS), (8, 256))

    def fold(value):
        return jnp.sum(value.reshape(TILE // 8, 8, 256), axis=0)

    zero = jnp.zeros((8, 256), F32)

    def forward(g):
        for n, (at, depth) in enumerate(((0, 768), (768, 768), (1536, 768), (2304, 576))):
            part = jnp.dot(un[:, at:at + depth], dense[g, at:at + depth], preferred_element_type=F32)
            if n:
                logits[g] += part
            else:
                logits[g] = part

        def body(i, carry):
            rows = pl.ds(pl.multiple_of(i * TILE, TILE), TILE)
            value = logits[g, rows] * inv[g, 0:1]
            logits[g, rows] = value
            return carry + fold(jnp.exp(value))

        sums = jnp.sum(lax.fori_loop(0, SHARD // TILE, body, zero), axis=0, keepdims=True)
        zx[g, 0] = jnp.concatenate([sums[:, 0:128], sums[:, 128:256]], axis=0)

    def zx_copy(g, k):
        return remote(zx.at[g, 0], zx.at[g, k], zx_s.at[0], zx_r.at[g], (layer, (voc + k) % 16))

    def zz_copy(g, k):
        return remote(zz.at[g, 0], zz.at[g, k], zz_s.at[0], zz_r.at[g], ((layer + k) % 16, voc))

    def all_of(copy, g):
        each(1, 16, lambda k: copy(g, k).start())


    eye = (lax.broadcasted_iota(jnp.int32, (256, 256), 0)
           == lax.broadcasted_iota(jnp.int32, (256, 256), 1)).astype(BF16)

    def turn(i):
        at = pl.multiple_of(i * 256, 256)
        unt[pl.ds(at, 256), :] = lax.dot_general(
            eye, un[:, pl.ds(at, 256)], (((1,), (1,)), ((), ())),
            preferred_element_type=F32).astype(BF16)

    def turn_last():
        unt[2816:D, :] = lax.dot_general(
            eye[0:64, 0:64], un[:, 2816:D], (((1,), (1,)), ((), ())),
            preferred_element_type=F32).astype(BF16)

    gather_own(1)
    gather_own(0)
    gather_on(1)
    pltpu.make_async_copy(un_h, un, local.at[5]).wait()
    each(0, 4, turn)
    gather_on(0)
    each(4, 7, turn)
    gather_end(1)
    share_come(1)
    join(1)
    forward(1)
    all_of(zx_copy, 1)
    each(7, 11, turn)
    turn_last()
    gather_end(0)
    share_come(0)
    join(0)
    forward(0)
    all_of(zx_copy, 0)
    landed(zx.at[1, pl.ds(1, 15)], zx_r.at[1])
    zz[1, 0] = jnp.sum(zx[1], axis=0)
    all_of(zz_copy, 1)

    fint[...] = jnp.concatenate([final] * 4, axis=0).T
    most = jnp.maximum(jnp.max(stat[0], axis=0), jnp.max(stat[1], axis=0))[3:4]
    most = jnp.broadcast_to(jnp.maximum(most[:, 0:128], most[:, 128:256]), (8, 128))
    for turn_by in (32, 64):
        most = jnp.maximum(most, pltpu.roll(most, turn_by, axis=1))
    wide = jnp.concatenate([most, most], axis=1)[0:1]
    sums = jnp.zeros((1, 256), F32)
    for g in both:
        scaled = jnp.exp(stat[g, :, 3:4, :] - wide[None])
        part = (stat[g, :, 4:5, :] + stat[g, :, 5:6, :] + stat[g, :, 6:7, :]) * scaled
        sums += jnp.sum(part, axis=0)
    sums = jnp.broadcast_to(sums[:, 0:128] + sums[:, 128:256], (8, 128))
    for turn_by in (32, 64):
        sums += pltpu.roll(sums, turn_by, axis=1)
    final_lse = (most + jnp.log(sums))[0:1]

    landed(zx.at[0, pl.ds(1, 15)], zx_r.at[0])
    zz[0, 0] = jnp.sum(zx[0], axis=0)
    all_of(zz_copy, 0)

    lane128 = lax.broadcasted_iota(jnp.int32, (1, 128), 1)
    row8 = lax.broadcasted_iota(jnp.int32, (8, 256), 0)

    def log_total(g):
        value = jnp.log(jnp.sum(zz[g], axis=0))
        return jnp.concatenate([value[0:1], value[1:2]], axis=1)

    def slopes(g, lse, ahead):
        def body(i, carry):
            rows = pl.ds(pl.multiple_of(i * TILE, TILE), TILE)
            value = logits[g, rows]
            prob = jnp.exp(value - lse)
            target = jnp.exp(fint[rows] - final_lse)
            target = jnp.concatenate([target, target], axis=1)
            p0, p1 = prob[:, 0:128], prob[:, 128:256]
            if ahead is None:
                follow = jnp.where(lane128 < 96, p1 - pltpu.roll(p0, 96, axis=1), 0.0)
            else:
                border = jnp.exp(logits[1, rows, 0:128] - ahead[:, 0:128])
                follow = p1 - pltpu.roll(jnp.where(lane128 < 32, border, p0), 96, axis=1)
            slope = (prob - target) + jnp.concatenate([p0 - p1, follow], axis=1)
            grad[g, rows] = slope.astype(BF16)
            return carry + fold(slope * value)

        proj = jnp.sum(lax.fori_loop(0, SHARD // TILE, body, zero), axis=0, keepdims=True)
        high = proj.astype(BF16).astype(F32)
        return jnp.where(row8 == 0, high, proj - high)

    def product(g, tag, i):
        rows = pl.ds(pl.multiple_of(i * QUAD, 16), QUAD)
        value = jnp.dot(unt[rows, :], grad[g], preferred_element_type=F32)
        for w in range(4):
            one, two = value[STEP * w:STEP * w + HALF], value[STEP * w + HALF:STEP * w + WIN]
            if w < 2:
                two = jnp.concatenate([two[0:88], jnp.where(row8 < 2, tag, two[88:96])], axis=0)
            else:
                one = jnp.concatenate([jnp.where(row8 < 2, tag, one[0:8]), one[8:96]], axis=0)
            one, two = one.astype(BF16), two.astype(BF16)
            for p in both:
                gt[p, g, 0, i, w] = one[:, 128 * p:128 * p + 128]
                gt[p, g, 1, w, i] = two[:, 128 * p:128 * p + 128]

    def cross(g, h, d):
        i = (x + d) % 4
        src = gt.at[other, g, 0, i] if h == 0 else gt.at[other, g, 1, :, i]
        land = core_in.at[g, 0, i] if h == 0 else core_in.at[g, 1, :, i]
        return remote(src, land, ce_s.at[0], ce_r.at[g, d], sibling)

    def s_back(g, h, j, k):
        f, s = axes[h]
        to = (s + k) % 4
        if h == 0:
            n = (f + j) % 4
            return remote(gt.at[c, g, 0, n, to], sin.at[g, 0, k, n], ss_s.at[0], ss_r.at[g, 0],
                          place(h, f, to))
        return remote(gt.at[c, g, 1, :, to], sin.at[g, 1, k], ss_s.at[0], ss_r.at[g, 1],
                      place(h, f, to))

    def merge(g, d):
        i = (x + d) % 4
        landed(core_in.at[g, :, 0], ce_r.at[g, d])
        for w in range(4):
            gt[c, g, 0, i, w] = (gt[c, g, 0, i, w].astype(F32) + core_in[g, 0, i, w].astype(F32)).astype(BF16)
            gt[c, g, 1, w, i] = (gt[c, g, 1, w, i].astype(F32) + core_in[g, 1, w, i].astype(F32)).astype(BF16)
        for k in FAR:
            begin(s_back, g, 0, d, k)
        if d:
            begin(s_back, g, 1, 0, d)

    order = (2, 1, 3, 0)

    def backward(g, tag):
        for n, d in enumerate(order):
            product(g, tag, (x + d) % 4)
            for h in both:
                begin(cross, g, h, d)
            if n:
                merge(g, order[n - 1])
        merge(g, order[3])

    def f_back(g, h, k):
        f, s = axes[h]
        to = (f + k) % 4
        return remote(q.at[g, h, to], fzin.at[g, h, k], sf_s.at[0], sf_r.at[g, h], place(h, to, s))

    def scatter_s(g):
        for h in (1, 0):
            f, s = axes[h]
            landed(sin.at[g, h, pl.ds(1, 3)], ss_r.at[g, h])

            def total_of(n):
                value = gt[c, g, h, n, s].astype(F32)
                for k in (1, 2, 3):
                    value += sin[g, h, k, n].astype(F32)
                return value

            for k in FAR:
                n = (f + k) % 4
                q[g, h, n] = total_of(n).astype(BF16)
                begin(f_back, g, h, k)
            qown[g, h] = total_of(f)

    def fz_copy(g, k):
        to = 4 * g + k
        return remote(fz16.at[to], fzr.at[(to + 8 - z) % 8], fz_s.at[0], fz_r.at[0], (to * 2 + c, voc))

    def scatter_f(g):
        whole = []
        for h in both:
            landed(fzin.at[g, h, pl.ds(1, 3)], sf_r.at[g, h])
            whole.append(qown[g, h] + fzin[g, h, 1].astype(F32) + fzin[g, h, 2].astype(F32)
                         + fzin[g, h, 3].astype(F32))
        own_inv = jnp.where(c == 0, inv[g, :, 0:128], inv[g, :, 128:256])
        full = jnp.concatenate([*whole, own_inv, jnp.zeros((56, 128), F32)], axis=0).T
        fz32[4 * g:4 * g + 4] = full.reshape(4, ROWS, 256)
        fz16[4 * g:4 * g + 4] = full.reshape(4, ROWS, 256).astype(BF16)
        for k in range(4):
            @pl.when(z != 4 * g + k)
            def _():
                fz_copy(g, k).start()

    landed(zz.at[1, pl.ds(1, 15)], zz_r.at[1])
    lse1 = log_total(1)
    tag1 = slopes(1, lse1, None)
    backward(1, tag1)
    landed(zz.at[0, pl.ds(1, 15)], zz_r.at[0])
    tag0 = slopes(0, log_total(0), lse1)
    for n, d in enumerate(order):
        product(0, tag0, (x + d) % 4)
        for h in both:
            begin(cross, 0, h, d)
        if n == 1:
            scatter_s(1)
        if n:
            merge(0, order[n - 1])
    merge(0, order[3])
    scatter_f(1)
    scatter_s(0)
    scatter_f(0)

    grown = fz32[z]
    inv_col = grown[:, WIN:WIN + 1]
    landed(fzr.at[pl.ds(1, 7)], fz_r.at[0])
    for k in range(1, 8):
        grown += fzr[k].astype(F32)
    along = jnp.sum(jnp.where((lane == base) | (lane == base + 1), grown, 0.0), axis=1, keepdims=True)
    grown = pltpu.roll(grown, (256 - shift) % 256, axis=1)[:, 0:OWN]
    out_ref[...] = inv_col * gain[...] * grown - lens[:, 0:OWN] * (inv_col * inv_col * along / D)

    sent(zbuf.at[pl.ds(0, 7)], gz_s.at[0])
    sent(nt.at[c, :, :, 0, pl.ds(0, 3)], gf_s.at[0])
    sent(nt.at[c, :, :, pl.ds(0, 3)], gs_s.at[0])
    sent(nt.at[c], gc_s.at[0])
    sent(zx.at[:, pl.ds(1, 15)], zx_s.at[0])
    sent(zz.at[:, pl.ds(1, 15)], zz_s.at[0])
    sent(gt.at[other], ce_s.at[0])
    sent(gt.at[c, :, :, pl.ds(0, 3)], ss_s.at[0])
    sent(q.at[:, :, pl.ds(0, 3)], sf_s.at[0])
    sent(fz16.at[pl.ds(0, 7)], fz_s.at[0])


def weights(hid_ref, go_ref, out_ref, bias_ref):
    turned = go_ref[...].T
    bias_ref[...] = jnp.sum(go_ref[...], axis=0, keepdims=True)
    value = jnp.dot(turned.astype(BF16), hid_ref[...], preferred_element_type=F32)
    out_ref[...] = value.reshape(out_ref.shape)


def on_device(hidden, translator, bias, gain, unembed, final_logits):
    vmem, sem = pltpu.VMEM, pltpu.SemaphoreType.DMA
    anywhere = pl.BlockSpec(memory_space=pl.ANY)
    inside = pl.BlockSpec(memory_space=pltpu.VMEM)
    grad_out = pl.pallas_call(
        kernel,
        out_shape=jax.ShapeDtypeStruct((ROWS, OWN), F32),
        in_specs=[anywhere] * 6,
        out_specs=inside,
        scratch_shapes=[
            vmem((ROWS, D), BF16), vmem((ROWS, 3072), F32), vmem((OWN, D), BF16),
            vmem((1, OWN), F32), vmem((1, OWN), F32),
            vmem((SHARD, D), BF16), vmem((D, SHARD), BF16),
            vmem((ROWS, SHARD), BF16), vmem((SHARD, 128), F32),
            vmem((ROWS, 256), F32), vmem((8, ROWS, 256), BF16),
            vmem((2, 2, 2, 4, 4, HALF, 128), BF16), vmem((2, D, 256), BF16),
            vmem((2, 16, 8, 256), F32), vmem((2, SHARD, 256), F32), vmem((2, 8, 256), F32),
            vmem((2, SHARD, 256), BF16), vmem((2, 2, 2, 4, 4, HALF, 128), BF16),
            vmem((2, 2, 4, 4, HALF, 128), BF16),
            vmem((2, 16, 2, 128), F32), vmem((2, 16, 2, 128), F32),
            vmem((2, 2, 4, 4, HALF, 128), BF16),
            vmem((2, 2, 4, HALF, 128), BF16), vmem((2, 2, HALF, 128), F32),
            vmem((2, 2, 4, HALF, 128), BF16),
            vmem((8, ROWS, 256), F32), vmem((8, ROWS, 256), BF16), vmem((8, ROWS, 256), BF16),
            sem((6,)), sem((1,)), sem((2,)), sem((1,)), sem((2, 2, 3)),
            sem((1,)), sem((2, 2, 4)), sem((1,)), sem((2,)), sem((1,)), sem((2,)), sem((1,)), sem((2,)),
            sem((1,)), sem((2, 4)), sem((1,)), sem((2, 2)),
            sem((1,)), sem((2, 2)), sem((1,)), sem((1,)),
        ],
        compiler_params=pltpu.CompilerParams(
            collective_id=0, has_side_effects=True, vmem_limit_bytes=58 * 1024 * 1024),
    )(hidden[0], translator[0].T, bias, gain.reshape(1, OWN), unembed.T, final_logits)
    grad_translator, grad_bias = pl.pallas_call(
        weights,
        out_shape=(jax.ShapeDtypeStruct((OWN, 1, D), F32), jax.ShapeDtypeStruct((1, OWN), F32)),
        in_specs=[inside, inside],
        out_specs=(inside, inside),
        compiler_params=pltpu.CompilerParams(vmem_limit_bytes=32 * 1024 * 1024),
    )(hidden[0], grad_out)
    return jnp.transpose(grad_translator, (1, 2, 0)), grad_bias


def solution(mesh):
    placed = (
        P("layer", None, None),
        P("layer", None, "vocab"),
        P("layer", "vocab"),
        P("vocab"),
        P(None, ("layer", "vocab")),
        P(None, ("layer", "vocab")),
    )
    return jax.shard_map(
        on_device,
        mesh=mesh,
        in_specs=placed,
        out_specs=(P("layer", None, "vocab"), P("layer", "vocab")),
        check_vma=False,
    )
```

time: 687 us -> 70.7 us (0.10)
  blocking collectives: 251 us -> 0 us
  waiting for transfers between devices: 248 us -> 0 us
  other arithmetic: 79.8 us -> 0 us
  Pallas kernels: 0 us -> 69.1 us
  local copies, waits for them, and re-layouts: 67.3 us -> 0.76 us
  matrix products: 18.3 us -> 0 us
  between operations: 13.9 us -> 0.66 us
    all_gather x1 -> x0, waiting for transfers between devices: 104 us -> none  [on_device(): lax.all_gather(normed[None], ('layer', 'vocab'), axis=0, tiled=True)]
    psum x3 -> x0, blocking collectives: 103 us -> none  [the longest x1 35 us: stats_narrow(): lax.psum((jnp.sum(jnp.exp(final_f32 - row_top[:, None]), axis=1), lens_to...]
    unnamed x4 -> x0, waiting for transfers between devices: 78.6 us -> none
    all_to_all x2 -> x0, blocking collectives: 78.2 us -> none  [the longest x1 49 us: on_device(): lax.all_to_all(logits, 'layer', split_axis=0, concat_axis=2, tiled=True)[0]]
    unnamed x1 -> x0, other arithmetic: 70.2 us -> none
    pallas_call x0 -> x2, Pallas kernels: none -> 69.1 us  [the longest x1 67.1 us: on_device(): pl.pallas_call(kernel, out_shape=jax.ShapeDtypeStruct((ROWS, OWN), F32),...]
    reduce_scatter x1 -> x0, waiting for transfers between devices: 63.2 us -> none  [on_device(): lax.psum_scatter(partial_value.astype(jnp.bfloat16), 'layer', scatter_dim...]
    all_gather x1 -> x0, blocking collectives: 36.1 us -> none  [on_device(): lax.all_gather(final_logits, 'layer', axis=1, tiled=True)]
  transfers between devices with their start and end apart: 5 -> 0, of which waited for: 4 -> 0; matrix products, arithmetic and copies ran while one was open for 4% -> 0% of each run, Pallas kernels for 0% -> 0%
where the time goes in v2:
time: 70.7 us; the launch traced here: 70.5 us
  Pallas kernels  69.1 us (98%)
  local copies, waits for them, and re-layouts  0.76 us (1%)
    pallas_call x1, Pallas kernels, on_device(): pl.pallas_call(kernel, out_shape=jax.ShapeDtypeStruct((ROWS, OWN), F32),...  67.1 us
    pallas_call x1, Pallas kernels, on_device(): pl.pallas_call(weights, out_shape=(jax.ShapeDtypeStruct((OWN, 1, D), F32)...  1.97 us

profile of v2, /device:TPU:2, one launch (start us, length us, event | category | flops | bytes accessed | tf_op | source)
XLA Modules:
  0.0 70.5 jit_solution(783590711542841880)
XLA Ops:
  0.6 0.0 copy-start
  0.6 67.1 %shard_map.77.go_ref = f32[32,180]{1,0:T(8,128)} custom-call(bf16[32,2880]{1,0:T(8,128)(2,1)} %bitcast.7, bf16[180,2880]{1,0:T(8,128)(2,1)} %bitcast.10, f32[1,180]{1,0:T(1,128)} %bias_h.1, f32[1,180]{1,0:T(1,128)} %bitcast.11, bf16[784,2880]{1,0:T(8,128)(2,1)} %bitcast.9, bf16[32,784]{1,0:T(8,128)(2,1)} %fin_h.1), custom_call_target="tpu_custom_call" | custom-call | tf_op jit(solution)/shard_map/pallas_call | solution.py:469
  67.7 0.0 copy-done
  67.7 0.0 copy-start.1
  67.8 0.7 %copy-done.1 = f32[32,180]{1,0:T(8,128)S(1)} copy-done((f32[32,180]{1,0:T(8,128)S(1)}, f32[32,180]{1,0:T(8,128)}, u32[]{:S(2)}) %copy-start.1) | copy-done | bytes 23064
  68.5 2.0 %shard_map.78 = (f32[180,1,2880]{2,1,0:T(1,128)}, f32[1,180]{1,0:T(1,128)}) custom-call(bf16[32,2880]{1,0:T(8,128)(2,1)S(1)} %bitcast.8, f32[32,180]{1,0:T(8,128)S(1)} %copy-done.1), custom_call_target="tpu_custom_call" | custom-call | tf_op jit(solution)/shard_map/pallas_call | solution.py:497
Async XLA Ops:
  0.6 67.1 %copy-start = (bf16[1,32,2880]{2,1,0:T(8,128)(2,1)S(1)}, bf16[1,32,2880]{2,1,0:T(8,128)(2,1)}, u32[]{:S(2)}) copy-start(bf16[1,32,2880]{2,1,0:T(8,128)(2,1)} %param.6) | copy-start | bytes 552964
  67.7 0.8 %copy-start.1 = (f32[32,180]{1,0:T(8,128)S(1)}, f32[32,180]{1,0:T(8,128)}, u32[]{:S(2)}) copy-start(f32[32,180]{1,0:T(8,128)} %shard_map.77.go_ref) | copy-start | bytes 69124

commit v3 on v2

--- a/solution.py
+++ b/solution.py
@@ -17,6 +17,8 @@
 TILE = 112
 NEAR = (1, 3, 2)
 FAR = (2, 1, 3)
+PLANE = (10, 9, 11, 6, 14, 5, 7, 8, 2, 13, 15, 1, 3, 4, 12)
+LINE = (8, 9, 7, 6, 10, 11, 5, 4, 12, 13, 3, 2, 14, 15, 1)
 
 
 def split3(value):
@@ -29,7 +31,7 @@
 def kernel(hid_h, trans_h, bias_h, gain_h, un_h, fin_h, out_ref,
            hid, hpad, trans, bias, gain, un, unt, fin, fint,
            lens, zbuf, nt, dense, stat, logits, inv, grad, gt, core_in,
-           zx, zz, sin, q, qown, fzin, fz32, fz16, fzr,
+           border, zx, zz, sin, q, qown, fzin, fz32, fz16, fzr,
            local, gz_s, gz_r, gf_s, gf_r, gs_s, gs_r, gc_s, gc_r, zx_s, zx_r, zz_s, zz_r,
            ce_s, ce_r, ss_s, ss_r, sf_s, sf_r, fz_s, fz_r):
     layer, voc = lax.axis_index("layer"), lax.axis_index("vocab")
@@ -171,18 +173,22 @@
                 for k in FAR:
                     begin(s_send, g, h, j, k)
 
+    def gather_end_part(g, n):
+        for h in both:
+            s_come(g, h, (0, *NEAR)[n])
+            begin(share, g, h, (0, *NEAR)[n])
+
     def gather_end(g):
-        for j in (0, *NEAR):
-            for h in both:
-                s_come(g, h, j)
-                begin(share, g, h, j)
+        for n in range(4):
+            gather_end_part(g, n)
 
     row16 = lax.broadcasted_iota(jnp.int32, (16, 128), 0)
 
-    def join(g):
+    def join(g, p):
+        cols = pl.ds(pl.multiple_of(128 * p, 128), 128)
+
         def body(i):
-            for p in both:
-                cols = slice(128 * p, 128 * p + 128)
+            if True:
                 for w in range(4):
                     at = pl.multiple_of(i * QUAD, 16) + STEP * w
                     head = nt[p, g, 0, i, w, 0:16]
@@ -202,6 +208,8 @@
                     stat[g, i * 4 + w, :, cols] = piece
 
         each(0, 4, body)
+
+    def norms(g):
         sums = jnp.sum(stat[g], axis=0)
         inv[g] = jnp.broadcast_to(lax.rsqrt((sums[0:1] + sums[1:2] + sums[2:3]) / D + EPS), (8, 256))
 
@@ -210,14 +218,15 @@
 
     zero = jnp.zeros((8, 256), F32)
 
-    def forward(g):
-        for n, (at, depth) in enumerate(((0, 768), (768, 768), (1536, 768), (2304, 576))):
-            part = jnp.dot(un[:, at:at + depth], dense[g, at:at + depth], preferred_element_type=F32)
-            if n:
-                logits[g] += part
-            else:
-                logits[g] = part
-
+    def product_of(g, n):
+        at, depth = ((0, 768), (768, 768), (1536, 768), (2304, 576))[n]
+        part = jnp.dot(un[:, at:at + depth], dense[g, at:at + depth], preferred_element_type=F32)
+        if n:
+            logits[g] += part
+        else:
+            logits[g] = part
+
+    def exps(g):
         def body(i, carry):
             rows = pl.ds(pl.multiple_of(i * TILE, TILE), TILE)
             value = logits[g, rows] * inv[g, 0:1]
@@ -234,7 +243,8 @@
         return remote(zz.at[g, 0], zz.at[g, k], zz_s.at[0], zz_r.at[g], ((layer + k) % 16, voc))
 
     def all_of(copy, g):
-        each(1, 16, lambda k: copy(g, k).start())
+        for k in PLANE if copy is zx_copy else LINE:
+            copy(g, k).start()
 
 
     eye = (lax.broadcasted_iota(jnp.int32, (256, 256), 0)
@@ -254,21 +264,26 @@
     gather_own(1)
     gather_own(0)
     gather_on(1)
+    gather_on(0)
     pltpu.make_async_copy(un_h, un, local.at[5]).wait()
     each(0, 4, turn)
-    gather_on(0)
-    each(4, 7, turn)
     gather_end(1)
+    join(1, c)
     share_come(1)
-    join(1)
-    forward(1)
+    join(1, other)
+    norms(1)
+    for n in range(4):
+        product_of(1, n)
+        gather_end_part(0, n)
+    exps(1)
     all_of(zx_copy, 1)
-    each(7, 11, turn)
-    turn_last()
-    gather_end(0)
+    join(0, c)
     share_come(0)
-    join(0)
-    forward(0)
+    join(0, other)
+    norms(0)
+    for n in range(4):
+        product_of(0, n)
+    exps(0)
     all_of(zx_copy, 0)
     landed(zx.at[1, pl.ds(1, 15)], zx_r.at[1])
     zz[1, 0] = jnp.sum(zx[1], axis=0)
@@ -290,6 +305,13 @@
         sums += pltpu.roll(sums, turn_by, axis=1)
     final_lse = (most + jnp.log(sums))[0:1]
 
+    def final_prob(i):
+        rows = pl.ds(pl.multiple_of(i * TILE, TILE), TILE)
+        fint[rows] = jnp.exp(fint[rows] - final_lse)
+
+    each(0, SHARD // TILE, final_prob)
+
+    each(4, 8, turn)
     landed(zx.at[0, pl.ds(1, 15)], zx_r.at[0])
     zz[0, 0] = jnp.sum(zx[0], axis=0)
     all_of(zz_copy, 0)
@@ -301,19 +323,18 @@
         value = jnp.log(jnp.sum(zz[g], axis=0))
         return jnp.concatenate([value[0:1], value[1:2]], axis=1)
 
-    def slopes(g, lse, ahead):
+    def slopes(g, lse):
         def body(i, carry):
             rows = pl.ds(pl.multiple_of(i * TILE, TILE), TILE)
             value = logits[g, rows]
             prob = jnp.exp(value - lse)
-            target = jnp.exp(fint[rows] - final_lse)
-            target = jnp.concatenate([target, target], axis=1)
+            target = jnp.concatenate([fint[rows], fint[rows]], axis=1)
             p0, p1 = prob[:, 0:128], prob[:, 128:256]
-            if ahead is None:
+            if g == 1:
                 follow = jnp.where(lane128 < 96, p1 - pltpu.roll(p0, 96, axis=1), 0.0)
+                border[rows] = p0
             else:
-                border = jnp.exp(logits[1, rows, 0:128] - ahead[:, 0:128])
-                follow = p1 - pltpu.roll(jnp.where(lane128 < 32, border, p0), 96, axis=1)
+                follow = p1 - pltpu.roll(jnp.where(lane128 < 32, border[rows], p0), 96, axis=1)
             slope = (prob - target) + jnp.concatenate([p0 - p1, follow], axis=1)
             grad[g, rows] = slope.astype(BF16)
             return carry + fold(slope * value)
@@ -415,23 +436,23 @@
             def _():
                 fz_copy(g, k).start()
 
+    each(8, 11, turn)
+    turn_last()
     landed(zz.at[1, pl.ds(1, 15)], zz_r.at[1])
-    lse1 = log_total(1)
-    tag1 = slopes(1, lse1, None)
+    tag1 = slopes(1, log_total(1))
     backward(1, tag1)
     landed(zz.at[0, pl.ds(1, 15)], zz_r.at[0])
-    tag0 = slopes(0, log_total(0), lse1)
+    tag0 = slopes(0, log_total(0))
     for n, d in enumerate(order):
         product(0, tag0, (x + d) % 4)
         for h in both:
             begin(cross, 0, h, d)
-        if n == 1:
-            scatter_s(1)
         if n:
             merge(0, order[n - 1])
     merge(0, order[3])
+    scatter_s(1)
+    scatter_s(0)
     scatter_f(1)
-    scatter_s(0)
     scatter_f(0)
 
     grown = fz32[z]
@@ -468,7 +489,7 @@
     inside = pl.BlockSpec(memory_space=pltpu.VMEM)
     grad_out = pl.pallas_call(
         kernel,
-        out_shape=jax.ShapeDtypeStruct((ROWS, OWN), F32),
+        out_shape=pltpu.VMEM((ROWS, OWN), F32),
         in_specs=[anywhere] * 6,
         out_specs=inside,
         scratch_shapes=[
@@ -481,7 +502,7 @@
             vmem((2, 16, 8, 256), F32), vmem((2, SHARD, 256), F32), vmem((2, 8, 256), F32),
             vmem((2, SHARD, 256), BF16), vmem((2, 2, 2, 4, 4, HALF, 128), BF16),
             vmem((2, 2, 4, 4, HALF, 128), BF16),
-            vmem((2, 16, 2, 128), F32), vmem((2, 16, 2, 128), F32),
+            vmem((SHARD, 128), F32), vmem((2, 16, 2, 128), F32), vmem((2, 16, 2, 128), F32),
             vmem((2, 2, 4, 4, HALF, 128), BF16),
             vmem((2, 2, 4, HALF, 128), BF16), vmem((2, 2, HALF, 128), F32),
             vmem((2, 2, 4, HALF, 128), BF16),

time: 70.7 us -> 66.7 us (0.943)
  Pallas kernels: 69.1 us -> 65.8 us
  local copies, waits for them, and re-layouts: 0.76 us -> 0.01 us
    pallas_call x1, Pallas kernels: 67.1 us -> 63.8 us  [on_device(): pl.pallas_call(kernel, out_shape=pltpu.VMEM((ROWS, OWN), F32), in_specs=[...]
    unnamed x4 -> x2, local copies, waits for them, and re-layouts: 0.76 us -> 0.01 us
where the time goes in v3:
time: 66.7 us; the launch traced here: 66.5 us
  Pallas kernels  65.8 us (99%)
    pallas_call x1, Pallas kernels, on_device(): pl.pallas_call(kernel, out_shape=pltpu.VMEM((ROWS, OWN), F32), in_specs=[...  63.8 us
    pallas_call x1, Pallas kernels, on_device(): pl.pallas_call(weights, out_shape=(jax.ShapeDtypeStruct((OWN, 1, D), F32)...  1.97 us

profile of v3, /device:TPU:2, one launch (start us, length us, event | category | flops | bytes accessed | tf_op | source)
XLA Modules:
  0.0 66.5 jit_solution(1709828634016362262)
XLA Ops:
  0.6 0.0 copy-start
  0.6 63.8 %shard_map.77.go_ref = f32[32,180]{1,0:T(8,128)S(1)} custom-call(bf16[32,2880]{1,0:T(8,128)(2,1)} %bitcast.7, bf16[180,2880]{1,0:T(8,128)(2,1)} %bitcast.10, f32[1,180]{1,0:T(1,128)} %bias_h.1, f32[1,180]{1,0:T(1,128)} %bitcast.11, bf16[784,2880]{1,0:T(8,128)(2,1)} %bitcast.9, bf16[32,784]{1,0:T(8,128)(2,1)} %fin_h.1), custom_call_target="tpu_custom_call" | custom-call | tf_op jit(solution)/shard_map/pallas_call | solution.py:490
  64.5 0.0 copy-done
  64.5 2.0 %shard_map.78 = (f32[180,1,2880]{2,1,0:T(1,128)}, f32[1,180]{1,0:T(1,128)}) custom-call(bf16[32,2880]{1,0:T(8,128)(2,1)S(1)} %bitcast.8, f32[32,180]{1,0:T(8,128)S(1)} %shard_map.77.go_ref), custom_call_target="tpu_custom_call" | custom-call | tf_op jit(solution)/shard_map/pallas_call | solution.py:518
Async XLA Ops:
  0.6 63.8 %copy-start = (bf16[1,32,2880]{2,1,0:T(8,128)(2,1)S(1)}, bf16[1,32,2880]{2,1,0:T(8,128)(2,1)}, u32[]{:S(2)}) copy-start(bf16[1,32,2880]{2,1,0:T(8,128)(2,1)} %param.6) | copy-start | bytes 552964

commit v4 on v3

--- a/solution.py
+++ b/solution.py
@@ -285,6 +285,7 @@
         product_of(0, n)
     exps(0)
     all_of(zx_copy, 0)
+    each(4, 6, turn)
     landed(zx.at[1, pl.ds(1, 15)], zx_r.at[1])
     zz[1, 0] = jnp.sum(zx[1], axis=0)
     all_of(zz_copy, 1)
@@ -311,7 +312,8 @@
 
     each(0, SHARD // TILE, final_prob)
 
-    each(4, 8, turn)
+    each(6, 11, turn)
+    turn_last()
     landed(zx.at[0, pl.ds(1, 15)], zx_r.at[0])
     zz[0, 0] = jnp.sum(zx[0], axis=0)
     all_of(zz_copy, 0)
@@ -391,9 +393,8 @@
             product(g, tag, (x + d) % 4)
             for h in both:
                 begin(cross, g, h, d)
-            if n:
-                merge(g, order[n - 1])
-        merge(g, order[3])
+            if n > 1:
+                merge(g, order[n - 2])
 
     def f_back(g, h, k):
         f, s = axes[h]
@@ -436,13 +437,13 @@
             def _():
                 fz_copy(g, k).start()
 
-    each(8, 11, turn)
-    turn_last()
     landed(zz.at[1, pl.ds(1, 15)], zz_r.at[1])
     tag1 = slopes(1, log_total(1))
     backward(1, tag1)
     landed(zz.at[0, pl.ds(1, 15)], zz_r.at[0])
+    merge(1, order[2])
     tag0 = slopes(0, log_total(0))
+    merge(1, order[3])
     for n, d in enumerate(order):
         product(0, tag0, (x + d) % 4)
         for h in both:

time: 66.7 us -> 65.4 us (0.981)
  Pallas kernels: 65.8 us -> 64.7 us
    pallas_call x1, Pallas kernels: 63.8 us -> 62.7 us  [on_device(): pl.pallas_call(kernel, out_shape=pltpu.VMEM((ROWS, OWN), F32), in_specs=[...]
where the time goes in v4:
time: 65.4 us; the launch traced here: 65.3 us
  Pallas kernels  64.7 us (99%)
  between operations  0.66 us (1%)
    pallas_call x1, Pallas kernels, on_device(): pl.pallas_call(kernel, out_shape=pltpu.VMEM((ROWS, OWN), F32), in_specs=[...  62.7 us
    pallas_call x1, Pallas kernels, on_device(): pl.pallas_call(weights, out_shape=(jax.ShapeDtypeStruct((OWN, 1, D), F32)...  1.97 us

profile of v4, /device:TPU:2, one launch (start us, length us, event | category | flops | bytes accessed | tf_op | source)
XLA Modules:
  0.0 65.3 jit_solution(10641737141480689263)
XLA Ops:
  0.6 0.0 copy-start
  0.6 62.7 %shard_map.77.go_ref = f32[32,180]{1,0:T(8,128)S(1)} custom-call(bf16[32,2880]{1,0:T(8,128)(2,1)} %bitcast.7, bf16[180,2880]{1,0:T(8,128)(2,1)} %bitcast.10, f32[1,180]{1,0:T(1,128)} %bias_h.1, f32[1,180]{1,0:T(1,128)} %bitcast.11, bf16[784,2880]{1,0:T(8,128)(2,1)} %bitcast.9, bf16[32,784]{1,0:T(8,128)(2,1)} %fin_h.1), custom_call_target="tpu_custom_call" | custom-call | tf_op jit(solution)/shard_map/pallas_call | solution.py:491
  63.3 0.0 copy-done
  63.3 2.0 %shard_map.78 = (f32[180,1,2880]{2,1,0:T(1,128)}, f32[1,180]{1,0:T(1,128)}) custom-call(bf16[32,2880]{1,0:T(8,128)(2,1)S(1)} %bitcast.8, f32[32,180]{1,0:T(8,128)S(1)} %shard_map.77.go_ref), custom_call_target="tpu_custom_call" | custom-call | tf_op jit(solution)/shard_map/pallas_call | solution.py:519
Async XLA Ops:
  0.6 62.7 %copy-start = (bf16[1,32,2880]{2,1,0:T(8,128)(2,1)S(1)}, bf16[1,32,2880]{2,1,0:T(8,128)(2,1)}, u32[]{:S(2)}) copy-start(bf16[1,32,2880]{2,1,0:T(8,128)(2,1)} %param.6) | copy-start | bytes 552964
